TPU v7x, 32 devices: a whole 2x2x4 slice. The times are simulated.
32 devices in a mesh: batch: 4 (over x, core), tensor: 8 (over z, y).
Axes of the slice: x: 2, y: 2, z: 4, core: 2. Of those that a mesh axis runs over, the one named last changes fastest.
Arguments:
- inputs: bfloat16 [4, 8, 32, 4096], P(None, 'batch', 'tensor'), may hold values from -6 to 6
- norm_gain: float32 [4096], replicated, may hold values from 0.5 to 1.5
- norm_bias: float32 [4096], replicated, may hold values from -3 to 3
- qkv_weight: bfloat16 [4096, 3, 4096], P(None, None, 'tensor'), may hold values from -0.09375 to 0.09375
- out_weight: bfloat16 [4096, 4096], P('tensor'), may hold values from -0.375 to 0.375
- in_weight: bfloat16 [4096, 8192], P(None, 'tensor'), may hold values from -0.09375 to 0.09375
- in_bias: float32 [8192], P('tensor'), may hold values from -3 to 3
- down_weight: bfloat16 [8192, 4096], P('tensor'), may hold values from -0.0625 to 0.0625
- down_bias: float32 [4096], replicated, may hold values from -3 to 3
- page_pool: bfloat16 [128, 2, 128, 4096], P('batch', None, None, 'tensor'), may hold values from -103 to 103
- old_cache: bfloat16 [8, 32, 2, 64, 4096], P('batch', None, None, None, 'tensor'), may hold values from -103 to 103, as said below
- page_table: int32 [32, 4], replicated, may hold values from 0 to 127, as said below
- prompt_length: int32 [32], replicated, may hold values from 1 to 512, 8192 in all
- parents: int32 [4, 8, 32], replicated, may hold values from 0 to 7
Outputs:
- outputs: float32 [4, 8, 32, 4096], P(None, 'batch', 'tensor')
Inputs may be any that keep to these rules, and one draw needn't show every extreme that they name: `old_cache`: key and value entries of the beams' generated tokens. `page_table`: every pool page is named exactly once in the table. The pool is cut into as many equal blocks of consecutive pages as the batch axis has devices; request r names only pages of block r modulo that count.
All inputs are finite; a program needn't handle non-finite values.
Results may differ from a plain program's by a relative error of at most 0.034.
Values may be sent and summed in bfloat16 or wider, within the bound.
A program may use at most 256 MiB of HBM per device.

v0:
```python
import math

import jax
import jax.numpy as jnp
from jax import lax
from jax.sharding import PartitionSpec as P

HDIM = 256
ROT = 64
BEAMS = 8
STEPS = 4


NEG_FILL = -1e30


def partner(value, axis, bit):
    return lax.ppermute(value, axis, [(i, i ^ 1 << bit) for i in range(lax.axis_size(axis))])


def joined_2(part, axis, combine):
    gathered = jax.tree.map(lambda a: lax.all_gather(a, axis), part)

    def take(source):
        return jax.tree.map(lambda a: lax.dynamic_index_in_dim(a, source, 0, False), gathered)

    return lax.fori_loop(
        1, lax.axis_size(axis), lambda source, state: combine(state, take(source)), take(0)
    )


def normalize(row_block, norm_gain, norm_bias):
    widened = row_block.astype(jnp.float32)
    center = jnp.mean(widened, axis=-1, keepdims=True)
    shifted = widened - center
    variance = jnp.mean(shifted * shifted, axis=-1, keepdims=True)
    return shifted * lax.rsqrt(variance + 1e-05) * norm_gain + norm_bias


def rotate_local(vectors, position, first_column):
    half_count = vectors.shape[-1] // 2
    doubled = (first_column + 2 * jnp.arange(half_count)) % HDIM
    exponent = doubled.astype(jnp.float32) / ROT
    frequency = jnp.where(doubled < ROT, jnp.exp(-exponent * math.log(10000.0)), 0.0)
    angles = position[:, None] * frequency[None, :]
    cosine = jnp.cos(angles)[None]
    sine_part = jnp.sin(angles)[None]
    halves = vectors.reshape(vectors.shape[:-1] + (half_count, 2))
    even_part = halves[..., 0]
    odd_part = halves[..., 1]
    turned = jnp.stack(
        [even_part * cosine - odd_part * sine_part, odd_part * cosine + even_part * sine_part],
        axis=-1,
    )
    return turned.reshape(vectors.shape)


def combine(earlier, later):
    peak_one, total_one, mixture_one = earlier
    peak_two, total_two, mixture_two = later
    peak = jnp.maximum(peak_one, peak_two)
    factor_one = jnp.exp(peak_one - peak)
    factor_two = jnp.exp(peak_two - peak)
    return (
        peak,
        total_one * factor_one + total_two * factor_two,
        mixture_one * factor_one[..., None] + mixture_two * factor_two[..., None],
    )


def partial_softmax(scores, allowed):
    masked = jnp.where(allowed, scores, NEG_FILL)
    peak = jnp.max(masked, axis=-1)
    weights = jnp.where(allowed, jnp.exp(masked - peak[..., None]), 0.0)
    return (peak, jnp.sum(weights, axis=-1), weights.astype(jnp.bfloat16))


def place_block(values, slot, slot_count, axis, fill_value):
    hit_shape = [1] * (values.ndim + 1)
    hit_shape[axis] = slot_count
    hits = (jnp.arange(slot_count) == slot).reshape(hit_shape)
    return jnp.where(hits, jnp.expand_dims(values, axis), fill_value)


def head_sum(prompt_scores, chain_scores, spread):
    for bit_index in range(spread.bit_length() - 1):
        other_prompt, other_chain = partner((prompt_scores, chain_scores), "tensor", bit_index)
        prompt_scores = prompt_scores + other_prompt
        chain_scores = chain_scores + other_chain
    return (prompt_scores, chain_scores)


def on_device(
    inputs,
    norm_gain,
    norm_bias,
    qkv_weight,
    out_weight,
    in_weight,
    in_bias,
    down_weight,
    down_bias,
    page_pool,
    old_cache,
    page_table,
    prompt_length,
    parents,
):
    batch_index = lax.axis_index("batch")
    tensor_index = lax.axis_index("tensor")
    groups = lax.axis_size("batch")
    beam_dev = inputs.shape[1]
    model_width = inputs.shape[3]
    columns = qkv_weight.shape[2]
    requests = page_table.shape[0]
    history = old_cache.shape[3]
    prompt_span = page_table.shape[1] * page_pool.shape[2]
    heads_dev = max(columns // HDIM, 1)
    head_part = min(columns, HDIM)
    spread = max(HDIM // columns, 1)
    scale_factor = HDIM ** (-0.5)
    qkv_flat = qkv_weight.reshape(model_width, 3 * columns)
    first_column = tensor_index * columns
    owners = batch_index * beam_dev + jnp.arange(beam_dev)
    old_keys = old_cache[:, :, 0].reshape(beam_dev, requests, history, heads_dev, head_part)
    old_values = old_cache[:, :, 1].reshape(beam_dev, requests, history, heads_dev, head_part)
    stored_keys = jnp.zeros((beam_dev, requests, STEPS, columns), jnp.bfloat16)
    stored_values = jnp.zeros((beam_dev, requests, STEPS, columns), jnp.bfloat16)
    beam_ids = jnp.broadcast_to(jnp.arange(BEAMS)[:, None], (BEAMS, requests))
    prompt_ok = jnp.arange(prompt_span)[None, :] < prompt_length[:, None]
    whole_pool = lax.all_gather(page_pool, "batch", axis=0, tiled=True)
    page_rows = whole_pool[page_table]
    count_rows = page_table.shape[0]
    prompt_keys = page_rows[:, :, 0].reshape(count_rows, prompt_span, heads_dev, head_part)
    prompt_values = page_rows[:, :, 1].reshape(count_rows, prompt_span, heads_dev, head_part)
    outputs = []
    for step_index in range(STEPS):
        current = inputs[step_index]
        normed = normalize(current, norm_gain, norm_bias).astype(jnp.bfloat16)
        gathered_rows = lax.all_gather(normed, "tensor", axis=1, tiled=True)
        attn_part = jnp.einsum(
            "brd,dc->brc", gathered_rows, qkv_flat, preferred_element_type=jnp.float32
        )
        ffn_part = jnp.einsum(
            "brd,dc->brc", gathered_rows, in_weight, preferred_element_type=jnp.float32
        )
        projected = jnp.concatenate([attn_part, ffn_part], axis=-1)
        position = (prompt_length + history + step_index).astype(jnp.float32)
        queries = rotate_local(projected[..., :columns], position, first_column).astype(
            jnp.bfloat16
        )
        fresh_keys = rotate_local(
            projected[..., columns : 2 * columns], position, first_column
        ).astype(jnp.bfloat16)
        fresh_values = projected[..., 2 * columns : 3 * columns].astype(jnp.bfloat16)
        hidden = jax.nn.gelu(projected[..., 3 * columns :] + in_bias, approximate=True).astype(
            jnp.bfloat16
        )
        stored_keys = stored_keys.at[:, :, step_index].set(fresh_keys)
        stored_values = stored_values.at[:, :, step_index].set(fresh_values)
        queries_all = lax.all_gather(queries, "batch", axis=0, tiled=True)
        query_heads = queries_all.reshape(BEAMS, requests, heads_dev, head_part)
        own_heads = queries.reshape(beam_dev, requests, heads_dev, head_part)
        ancestry = []
        lineage = beam_ids
        for back_step in range(step_index, -1, -1):
            ancestry.append(lineage)
            lineage = jnp.take_along_axis(parents[back_step], lineage, axis=0)
        unused_steps = [jnp.full_like(beam_ids, -1)] * (STEPS - 1 - step_index)
        ancestry_all = jnp.stack(ancestry[::-1] + unused_steps, axis=-1)
        stored_k = stored_keys.reshape(beam_dev, requests, STEPS, heads_dev, head_part)
        stored_v = stored_values.reshape(beam_dev, requests, STEPS, heads_dev, head_part)
        chain_scores = (
            jnp.concatenate(
                [
                    jnp.einsum(
                        "brnd,jrtnd->brnjt",
                        query_heads,
                        old_keys,
                        preferred_element_type=jnp.float32,
                    ),
                    jnp.einsum(
                        "brnd,jrtnd->brnjt",
                        query_heads,
                        stored_k,
                        preferred_element_type=jnp.float32,
                    ),
                ],
                axis=-1,
            )
            * scale_factor
        )
        old_ok = jnp.broadcast_to(
            (lineage[:, :, None] == owners[None, None, :])[:, :, :, None],
            (BEAMS, requests, beam_dev, history),
        )
        new_ok = ancestry_all[:, :, None, :] == owners[None, None, :, None]
        chain_ok = jnp.concatenate([old_ok, new_ok], axis=-1).reshape(BEAMS, requests, 1, -1)
        prompt_scores = (
            jnp.einsum(
                "brnd,rtnd->brnt", own_heads, prompt_keys, preferred_element_type=jnp.float32
            )
            * scale_factor
        )
        prompt_scores, chain_scores = head_sum(prompt_scores, chain_scores, spread)
        prompt_peak, prompt_total, prompt_weights = partial_softmax(
            prompt_scores, prompt_ok[None, :, None, :]
        )
        prompt_mix = jnp.einsum(
            "brnt,rtnd->brnd", prompt_weights, prompt_values, preferred_element_type=jnp.float32
        )
        peak_full = place_block(prompt_peak, batch_index, groups, 0, NEG_FILL).reshape(
            BEAMS, requests, heads_dev
        )
        total_full = place_block(prompt_total, batch_index, groups, 0, 0.0).reshape(
            BEAMS, requests, heads_dev
        )
        mix_full = place_block(prompt_mix, batch_index, groups, 0, 0.0).reshape(
            BEAMS, requests, heads_dev, head_part
        )
        chain_peak, chain_total, chain_weights = partial_softmax(
            chain_scores.reshape(BEAMS, requests, heads_dev, -1), chain_ok
        )
        chain_weights = chain_weights.reshape(BEAMS, requests, heads_dev, beam_dev, history + STEPS)
        chain_mix = jnp.einsum(
            "brnjt,jrtnd->brnd",
            chain_weights[..., :history],
            old_values,
            preferred_element_type=jnp.float32,
        )
        chain_mix = chain_mix + jnp.einsum(
            "brnjt,jrtnd->brnd",
            chain_weights[..., history:],
            stored_v,
            preferred_element_type=jnp.float32,
        )
        joined = combine((peak_full, total_full, mix_full), (chain_peak, chain_total, chain_mix))
        merged = joined_2((joined[0], joined[1], joined[2]), "batch", combine)
        first_beam = batch_index * beam_dev
        total_own = lax.dynamic_slice_in_dim(merged[1], first_beam, beam_dev, 0)
        mix_own = lax.dynamic_slice_in_dim(merged[2], first_beam, beam_dev, 0)
        attention = (
            (mix_own / total_own[..., None])
            .reshape(beam_dev, requests, columns)
            .astype(jnp.bfloat16)
        )
        summed = lax.psum_scatter(
            jnp.einsum("brc,cd->rbd", attention, out_weight, preferred_element_type=jnp.float32)
            + jnp.einsum("brf,fd->rbd", hidden, down_weight, preferred_element_type=jnp.float32),
            "tensor",
            scatter_dimension=0,
            tiled=True,
        )
        update = jnp.transpose(summed, (1, 0, 2))
        result = current.astype(jnp.float32) + update + down_bias
        outputs.append(result)
    return jnp.stack(outputs, axis=0)


def solution(mesh):
    in_specs = (
        P(None, "batch", "tensor", None),
        P(),
        P(),
        P(None, None, "tensor"),
        P("tensor", None),
        P(None, "tensor"),
        P("tensor"),
        P("tensor", None),
        P(),
        P("batch", None, None, "tensor"),
        P("batch", None, None, None, "tensor"),
        P(),
        P(),
        P(),
    )
    out_specs = P(None, "batch", "tensor", None)
    return jax.shard_map(
        on_device, mesh=mesh, in_specs=in_specs, out_specs=out_specs, check_vma=False
    )
```

profile of v0, /device:TPU:0, one launch (start us, length us, event | category | flops | bytes accessed | tf_op | source)
XLA Modules:
  0.0 863.5 jit_solution(5039582695419550062)
XLA Ops:
  30.0 9.3 %fusion.456 = (bf16[2,32,1,64,512]{4,3,2,1,0:T(8,128)(2,1)}, bf16[2,32,1,64,512]{4,3,2,1,0:T(8,128)(2,1)}) fusion(bf16[2,32,2,64,512]{4,3,2,1,0:T(8,128)(2,1)} %param.50), kind=kLoop, calls=%fused_computation.555 | loop fusion | bytes 16777216 | tf_op jit(solution)/shard_map/slice | solution.py:126
  39.3 7.0 reshape_squeeze.15
  53.2 17.0 %copy.737 = bf16[4096,3,512]{0,2,1:T(8,128)(2,1)} copy(bf16[4096,3,512]{2,0,1:T(8,128)(2,1)} %param.43) | data formatting | bytes 25165824 | tf_op args[3]
  72.4 33.1 %all_gather.84 = bf16[2,32,4096]{2,0,1:T(2,128)(2,1)S(1)} all-gather(bf16[2,4,4096]{2,0,1:T(2,128)(2,1)S(1)} %get-tuple-element.1143), channel_id=1, replica_groups=mesh['batch'=4,'tensor'=8] {'tensor'}, dimensions={1}, use_global_device_ids=true | all-gather | bytes 589824 | tf_op jit(solution)/shard_map/all_gather | solution.py:140
  105.6 8.5 fusion.210
  114.9 31.4 %all_gather.90 = bf16[2,32,4096]{2,0,1:T(2,128)(2,1)S(1)} all-gather(bf16[2,4,4096]{2,0,1:T(2,128)(2,1)S(1)} %get-tuple-element.1141), channel_id=1, replica_groups=mesh['batch'=4,'tensor'=8] {'tensor'}, dimensions={1}, use_global_device_ids=true | all-gather | bytes 589824 | tf_op jit(solution)/shard_map/all_gather | solution.py:140
  146.3 8.7 %fusion.207 = f32[2,32,1536]{2,1,0:T(8,128)S(1)} fusion(bf16[4096,1536,1]{0,1,2:T(8,128)(2,1)} %bitcast.610, bf16[2,32,4096]{2,0,1:T(2,128)(2,1)S(1)} %all_gather.90), kind=kOutput, calls=%fused_computation.193 | convolution fusion | flops 805306368 | bytes 13500416 | tf_op jit(solution)/shard_map/brd,dc->brc/dot_general | solution.py:141
  155.8 31.5 %all_gather.96 = bf16[2,32,4096]{2,0,1:T(2,128)(2,1)S(1)} all-gather(bf16[2,4,4096]{2,0,1:T(2,128)(2,1)S(1)} %get-tuple-element.1140), channel_id=1, replica_groups=mesh['batch'=4,'tensor'=8] {'tensor'}, dimensions={1}, use_global_device_ids=true | all-gather | bytes 589824 | tf_op jit(solution)/shard_map/all_gather | solution.py:140
  187.2 9.1 %fusion.204 = f32[2,32,1536]{2,1,0:T(8,128)S(1)} fusion(bf16[4096,1536,1]{0,1,2:T(8,128)(2,1)} %bitcast.611, bf16[2,32,4096]{2,0,1:T(2,128)(2,1)S(1)} %all_gather.96), kind=kOutput, calls=%fused_computation.190 | convolution fusion | flops 805306368 | bytes 13500416 | tf_op jit(solution)/shard_map/brd,dc->brc/dot_general | solution.py:141
  197.1 31.5 %all_gather.102 = bf16[2,32,4096]{2,0,1:T(2,128)(2,1)S(1)} all-gather(bf16[2,4,4096]{2,0,1:T(2,128)(2,1)S(1)} %get-tuple-element.1142), channel_id=1, replica_groups=mesh['batch'=4,'tensor'=8] {'tensor'}, dimensions={1}, use_global_device_ids=true | all-gather | bytes 589824 | tf_op jit(solution)/shard_map/all_gather | solution.py:140
  228.6 8.7 %fusion.201 = f32[2,32,1536]{2,1,0:T(8,128)S(1)} fusion(bf16[4096,1536,1]{0,1,2:T(8,128)(2,1)} %bitcast.612, bf16[2,32,4096]{2,0,1:T(2,128)(2,1)S(1)} %all_gather.102), kind=kOutput, calls=%fused_computation.187 | convolution fusion | flops 805306368 | bytes 13500416 | tf_op jit(solution)/shard_map/brd,dc->brc/dot_general | solution.py:141
  352.3 10.0 %fusion.42 = f32[2,32,4096]{2,1,0:T(8,128)} fusion(bf16[1024,4096]{1,0:T(8,128)(2,1)} %param.47, bf16[4096,1024]{1,0:T(8,128)(2,1)} %param.45, bf16[2,32,4096]{2,0,1:T(2,128)(2,1)S(1)} %all_gather.84, f32[1024]{0:T(1024)S(1)} %copy-done.44), kind=kOutput, calls=%fused_computation.87 | convolution fusion | flops 1074397184 | bytes 18354176 | tf_op jit(solution)/shard_map/brf,fd->rbd/dot_general | solution.py:249
  362.3 23.0 %gather_fusion = bf16[128,2,128,512]{3,2,1,0:T(8,128)(2,1)} fusion(bf16[128,2,128,512]{3,2,1,0:T(8,128)(2,1)} %all-gather.10.cloned.1.call-done, s32[1024]{0:T(1024)S(1)} %pad_clamp_fusion), kind=kCustom, calls=%fused_computation.10 | custom fusion | bytes 67109376 | tf_op jit(solution)/shard_map/gather | solution.py:132
  385.3 23.0 %slice_bitcast_fusion = (bf16[32,4,1,128,512]{4,3,1,0,2:T(8,128)(2,1)}, bf16[32,4,1,128,512]{4,3,1,0,2:T(8,128)(2,1)}) fusion(bf16[32,4,2,128,512]{4,3,2,1,0:T(8,128)(2,1)} %bitcast.613), kind=kLoop, calls=%fused_computation.63 | loop fusion | bytes 67108864
  408.3 23.7 %reshape_squeeze.14 = bf16[32,512,2,256]{3,2,1,0:T(2,128)(2,1)} reshape(bf16[32,4,1,128,512]{4,3,1,0,2:T(8,128)(2,1)} %get-tuple-element.1076) | data formatting | bytes 33554432 | tf_op jit(solution)/shard_map/reshape;squeeze | solution.py:135
  432.0 23.7 %reshape_squeeze.12 = bf16[32,512,2,256]{3,2,1,0:T(2,128)(2,1)} reshape(bf16[32,4,1,128,512]{4,3,1,0,2:T(8,128)(2,1)} %get-tuple-element.1077) | data formatting | bytes 33554432 | tf_op jit(solution)/shard_map/reshape;squeeze | solution.py:134
  455.8 10.0 %fusion.463 = (f32[2,32,2]{0,2,1:T(2,128)S(1)}, f32[2,32,2,512]{3,0,2,1:T(2,128)S(1)}) fusion(bf16[2,32,2,256]{3,0,2,1:T(2,128)(2,1)S(1)} %copy-done.49, bf16[32,512,2,256]{3,2,1,0:T(2,128)(2,1)} %reshape_squeeze.12, pred[32,512]{1,0:T(8,128)(4,1)S(1)} %iota_compare_fusion), kind=kOutput, calls=%fused_computation.562 | convolution fusion | flops 33750912 | bytes 17121792 | tf_op jit(solution)/shard_map/brnd,rtnd->brnt/dot_general | solution.py:200
  465.9 10.6 %fusion.464 = (f32[2,32,2]{0,2,1:T(2,128)S(1)}, f32[2,32,2,512]{3,0,2,1:T(2,128)}) fusion(bf16[2,32,2,256]{3,0,2,1:T(2,128)(2,1)S(1)} %copy-done.48, bf16[32,512,2,256]{3,2,1,0:T(2,128)(2,1)} %reshape_squeeze.12, pred[32,512]{1,0:T(8,128)(4,1)S(1)} %iota_compare_fusion), kind=kOutput, calls=%fused_computation.563 | convolution fusion | flops 33750912 | bytes 17121792 | tf_op jit(solution)/shard_map/brnd,rtnd->brnt/dot_general | solution.py:200
  476.5 10.6 %fusion.465 = (f32[2,32,2]{0,2,1:T(2,128)S(1)}, f32[2,32,2,512]{3,0,2,1:T(2,128)}) fusion(bf16[2,32,2,256]{3,0,2,1:T(2,128)(2,1)S(1)} %copy-done.47, bf16[32,512,2,256]{3,2,1,0:T(2,128)(2,1)} %reshape_squeeze.12, pred[32,512]{1,0:T(8,128)(4,1)S(1)} %iota_compare_fusion), kind=kOutput, calls=%fused_computation.564 | convolution fusion | flops 33750912 | bytes 17121792 | tf_op jit(solution)/shard_map/brnd,rtnd->brnt/dot_general | solution.py:200
  487.1 10.8 %fusion.462 = (f32[2,32,2]{0,2,1:T(2,128)S(1)}, f32[2,32,2,512]{3,0,2,1:T(2,128)}) fusion(bf16[2,32,2,256]{3,0,2,1:T(2,128)(2,1)S(1)} %copy-done.50, bf16[32,512,2,256]{3,2,1,0:T(2,128)(2,1)} %reshape_squeeze.12, pred[32,512]{1,0:T(8,128)(4,1)S(1)} %iota_compare_fusion), kind=kOutput, calls=%fused_computation.561 | convolution fusion | flops 33750912 | bytes 17121792 | tf_op jit(solution)/shard_map/brnd,rtnd->brnt/dot_general | solution.py:200
  499.2 8.1 fusion.163
  512.3 8.9 %fusion.36 = f32[2,32,4096]{2,1,0:T(8,128)S(1)} fusion(bf16[1024,4096]{1,0:T(8,128)(2,1)} %param.47, bf16[4096,1024]{1,0:T(8,128)(2,1)} %param.45, bf16[2,32,4096]{2,0,1:T(2,128)(2,1)S(1)} %copy-done.6, f32[1024]{0:T(1024)S(1)} %copy-done.45), kind=kOutput, calls=%fused_computation.81 | convolution fusion | flops 1074397184 | bytes 18354176 | tf_op jit(solution)/shard_map/brf,fd->rbd/dot_general | solution.py:249
  521.3 9.0 %fusion.40 = f32[2,32,4096]{2,1,0:T(8,128)S(1)} fusion(bf16[1024,4096]{1,0:T(8,128)(2,1)} %param.47, bf16[4096,1024]{1,0:T(8,128)(2,1)} %param.45, bf16[2,32,4096]{2,0,1:T(2,128)(2,1)S(1)} %copy-done.4, f32[1024]{0:T(1024)S(1)} %copy-done.46), kind=kOutput, calls=%fused_computation.85 | convolution fusion | flops 1074397184 | bytes 18354176 | tf_op jit(solution)/shard_map/brf,fd->rbd/dot_general | solution.py:249
  531.7 8.2 fusion.166
  545.5 10.0 %fusion.38 = f32[2,32,4096]{2,1,0:T(8,128)} fusion(bf16[1024,4096]{1,0:T(8,128)(2,1)} %param.47, bf16[4096,1024]{1,0:T(8,128)(2,1)} %param.45, bf16[2,32,4096]{2,0,1:T(2,128)(2,1)S(1)} %copy-done.2, f32[1024]{0:T(1024)} %param.46), kind=kOutput, calls=%fused_computation.83 | convolution fusion | flops 1074397184 | bytes 18354176 | tf_op jit(solution)/shard_map/brf,fd->rbd/dot_general | solution.py:249
  569.6 8.1 fusion.169
  623.6 8.2 fusion.160
  637.7 9.6 %while.85 = (s32[]{:T(128)}, f32[8,32,2]{1,2,0:T(2,128)S(1)}, f32[8,32,2]{1,2,0:T(2,128)S(1)}, f32[8,32,2,256]{3,2,1,0:T(2,128)S(1)}, f32[4,8,32,2]{2,1,3,0:T(8,...) while((s32[]{:T(128)}, f32[8,32,2]{1,2,0:T(2,128)S(1)}, ...), condition=%wide.region_16.18_spmd, body=%wide.region_15.17_spmd.sunk | while | flops 396293 | bytes 2658447 | solution.py:27
  648.7 9.6 %while.86 = (s32[]{:T(128)}, f32[8,32,2]{1,2,0:T(2,128)S(1)}, f32[8,32,2]{1,2,0:T(2,128)S(1)}, f32[8,32,2,256]{3,2,1,0:T(2,128)S(1)}, f32[4,8,32,2]{2,1,3,0:T(8,...) while((s32[]{:T(128)}, f32[8,32,2]{1,2,0:T(2,128)S(1)}, ...), condition=%wide.region_25.27_spmd, body=%wide.region_24.26_spmd.sunk | while | flops 396293 | bytes 2658447 | solution.py:27
  660.4 9.6 %while.87 = (s32[]{:T(128)}, f32[8,32,2]{1,2,0:T(2,128)S(1)}, f32[8,32,2]{1,2,0:T(2,128)S(1)}, f32[8,32,2,256]{3,2,1,0:T(2,128)S(1)}, f32[4,8,32,2]{2,1,3,0:T(8,...) while((s32[]{:T(128)}, f32[8,32,2]{1,2,0:T(2,128)S(1)}, ...), condition=%wide.region_34.36_spmd, body=%wide.region_33.35_spmd.sunk | while | flops 396293 | bytes 2658447 | solution.py:27
  671.7 7.5 while.84
  693.2 157.2 %all-reduce.9.cloned.1.call-done = (f32[32,2,4096]{2,0,1:T(8,128)}, f32[32,2,4096]{2,0,1:T(8,128)}, f32[32,2,4096]{2,0,1:T(8,128)}, f32[32,2,4096]{2,0,1:T(8,128)}) async-done(((f32[32,2,4096]{2,0,1:T(8,128)}, f32[32,2,4096]{2,0,1:T(8,128)}, f32[32,2,4096]{2,0,1:T(8,128)}, f32[32,2,4096]{2,0,1:T(8,128)}), (f32[32,2,4096]{2,0,1:T(8,128)}, f32[32,2,4096]{2,0,1:T(8,128)}, f32[32,2,4096]{2,0,1:T(8,128)}, ...) | async-done | bytes 4194320
  (536 shorter events, 288.2 us)
Async XLA Ops:
  6.5 355.7 %all-gather.10.cloned.1.call-start = ((), (), s32[]{:S(2)}) async-start(), calls=%async_computation | async-start | bytes 41943040 | tf_op jit(solution)/shard_map/all_gather | solution.py:131
  7.3 629.0 %all-gather.14.cloned.1.call-start = ((), (), s32[]{:S(2)}) async-start(), calls=%async_computation.2 | async-start | bytes 2621440 | tf_op jit(solution)/shard_map/all_gather | solution.py:22
  53.2 17.0 %copy-start.17 = (bf16[4,2,4,4096]{3,2,1,0:T(4,128)(2,1)S(1)}, bf16[4,2,4,4096]{3,2,1,0:T(4,128)(2,1)}, u32[]{:S(2)}) copy-start(bf16[4,2,4,4096]{3,2,1,0:T(4,128)(2,1)} %param.40) | copy-start | bytes 786436
  53.2 18.6 %copy-start.59 = (f32[4096]{0:T(1024)S(1)}, f32[4096]{0:T(1024)}, u32[]{:S(2)}) copy-start(f32[4096]{0:T(1024)} %param.42) | copy-start | bytes 49156
  53.2 18.6 %copy-start.60 = (f32[4096]{0:T(1024)S(1)}, f32[4096]{0:T(1024)}, u32[]{:S(2)}) copy-start(f32[4096]{0:T(1024)} %param.41) | copy-start | bytes 49156
  70.3 35.2 %copy-start.13 = (bf16[1,2,4,4096]{3,2,1,0:T(4,128)(2,1)}, bf16[1,2,4,4096]{3,2,1,0:T(4,128)(2,1)S(1)}, u32[]{:S(2)}) copy-start(bf16[1,2,4,4096]{3,2,1,0:T(4,128)(2,1)S(1)} %get-tuple-element.1138) | copy-start | bytes 196612
  70.3 35.2 %copy-start.15 = (bf16[1,2,4,4096]{3,2,1,0:T(4,128)(2,1)}, bf16[1,2,4,4096]{3,2,1,0:T(4,128)(2,1)S(1)}, u32[]{:S(2)}) copy-start(bf16[1,2,4,4096]{3,2,1,0:T(4,128)(2,1)S(1)} %get-tuple-element.1139) | copy-start | bytes 196612
  319.5 17.7 %copy-start.32 = (pred[8,32,2,4]{3,0,2,1:T(8,128)(4,1)S(1)}, pred[8,32,2,4]{3,0,2,1:T(8,128)(4,1)}, u32[]{:S(2)}) copy-start(pred[8,32,2,4]{3,0,2,1:T(8,128)(4,1)} %get-tuple-element.1209) | copy-start | bytes 6148
  329.4 17.0 %copy-start.19 = (bf16[2,32,4,2,256]{4,3,1,0,2:T(2,128)(2,1)S(1)}, bf16[2,32,4,2,256]{4,3,1,0,2:T(2,128)(2,1)}, u32[]{:S(2)}) copy-start(bf16[2,32,4,2,256]{4,3,1,0,2:T(2,128)(2,1)} %reshape.1196) | copy-start | bytes 786436
  333.6 18.6 %copy-start.65 = (s32[32]{0:T(128)S(1)}, s32[32]{0:T(128)}, u32[]{:S(2)}) copy-start(s32[32]{0:T(128)} %param.52) | copy-start | bytes 388
  333.6 18.7 %copy-start.44 = (f32[1024]{0:T(1024)S(1)}, f32[1024]{0:T(1024)}, u32[]{:S(2)}) copy-start(f32[1024]{0:T(1024)} %param.46) | copy-start | bytes 12292
  343.1 155.1 %copy-start.39 = (f32[8,32,2]{1,0,2:T(8,128)}, f32[8,32,2]{1,0,2:T(8,128)S(1)}, u32[]{:S(2)}) copy-start(f32[8,32,2]{1,0,2:T(8,128)S(1)} %copy.847) | copy-start | bytes 6148
  343.6 18.7 %copy-start.27 = (bf16[8,32,2,2,68]{4,0,3,2,1:T(8,128)(2,1)}, bf16[8,32,2,2,68]{4,0,3,2,1:T(8,128)(2,1)S(1)}, u32[]{:S(2)}) copy-start(bf16[8,32,2,2,68]{4,0,3,2,1:T(8,128)(2,1)S(1)} %get-tuple-element.1084) | copy-start | bytes 417796
  352.3 146.9 %copy-start.51 = (pred[32,512]{1,0:T(8,128)(4,1)}, pred[32,512]{1,0:T(8,128)(4,1)S(1)}, u32[]{:S(2)}) copy-start(pred[32,512]{1,0:T(8,128)(4,1)S(1)} %iota_compare_fusion) | copy-start | bytes 49156
  432.0 23.7 %copy-start.49 = (bf16[2,32,2,256]{3,0,2,1:T(2,128)(2,1)S(1)}, bf16[2,32,2,256]{3,0,2,1:T(2,128)(2,1)}, u32[]{:S(2)}) copy-start(bf16[2,32,2,256]{3,0,2,1:T(2,128)(2,1)} %copy.791) | copy-start | bytes 196612
  465.8 33.4 %copy-start.29 = (f32[2,32,2,512]{3,0,2,1:T(2,128)}, f32[2,32,2,512]{3,0,2,1:T(2,128)S(1)}, u32[]{:S(2)}) copy-start(f32[2,32,2,512]{3,0,2,1:T(2,128)S(1)} %get-tuple-element.1219) | copy-start | bytes 786436
  498.0 57.5 %copy-start.37 = (f32[2,32,2]{0,2,1:T(2,128)}, f32[2,32,2]{0,2,1:T(2,128)S(1)}, u32[]{:S(2)}) copy-start(f32[2,32,2]{0,2,1:T(2,128)S(1)} %get-tuple-element.1216) | copy-start | bytes 1540
  511.7 135.6 %all-gather.16.cloned.1.call-start = ((), (), s32[]{:S(2)}) async-start(), calls=%async_computation.3 | async-start | bytes 2621440 | tf_op jit(solution)/shard_map/all_gather | solution.py:22
  545.3 113.7 %all-gather.18.cloned.1.call-start = ((), (), s32[]{:S(2)}) async-start(), calls=%async_computation.4 | async-start | bytes 2621440 | tf_op jit(solution)/shard_map/all_gather | solution.py:22
  577.7 15.2 %copy-start.56 = (f32[1,8,32,2]{2,1,3,0:T(8,128)S(1)}, f32[1,8,32,2]{2,1,3,0:T(8,128)}, u32[]{:S(2)}) copy-start(f32[1,8,32,2]{2,1,3,0:T(8,128)} %get-tuple-element.1198) | copy-start | bytes 6148
  577.7 20.4 %copy-start.55 = (f32[1,8,32,2]{2,1,3,0:T(8,128)S(1)}, f32[1,8,32,2]{2,1,3,0:T(8,128)}, u32[]{:S(2)}) copy-start(f32[1,8,32,2]{2,1,3,0:T(8,128)} %get-tuple-element.1199) | copy-start | bytes 6148
  577.7 33.3 %copy-start.54 = (f32[1,8,32,2]{2,1,3,0:T(8,128)S(1)}, f32[1,8,32,2]{2,1,3,0:T(8,128)}, u32[]{:S(2)}) copy-start(f32[1,8,32,2]{2,1,3,0:T(8,128)} %get-tuple-element.1201) | copy-start | bytes 6148
  577.7 45.9 %copy-start.53 = (pred[32,512]{1,0:T(8,128)(4,1)S(1)}, pred[32,512]{1,0:T(8,128)(4,1)}, u32[]{:S(2)}) copy-start(pred[32,512]{1,0:T(8,128)(4,1)} %copy-done.51) | copy-start | bytes 49156
  587.6 82.8 %all-gather.12.cloned.1.call-start = ((), (), s32[]{:S(2)}) async-start(), calls=%async_computation.1 | async-start | bytes 2621440 | tf_op jit(solution)/shard_map/all_gather | solution.py:22
  592.8 18.2 %copy-start.35 = (f32[4,8,32,2]{2,1,3,0:T(8,128)}, f32[4,8,32,2]{2,1,3,0:T(8,128)S(1)}, u32[]{:S(2)}) copy-start(f32[4,8,32,2]{2,1,3,0:T(8,128)S(1)} %all_gather.92) | copy-start | bytes 24580
  598.0 18.2 %copy-start.36 = (f32[4,8,32,2]{2,1,3,0:T(8,128)}, f32[4,8,32,2]{2,1,3,0:T(8,128)S(1)}, u32[]{:S(2)}) copy-start(f32[4,8,32,2]{2,1,3,0:T(8,128)S(1)} %all_gather.93) | copy-start | bytes 24580
  636.2 214.1 %all-reduce.9.cloned.1.call-start = ((), (), s32[]{:S(2)}) async-start(), calls=%async_computation.5 | async-start | bytes 8388608
  688.1 166.2 %copy-start.10 = (bf16[1,2,4,4096]{3,2,1,0:T(4,128)(2,1)S(1)}, bf16[1,2,4,4096]{3,2,1,0:T(4,128)(2,1)}, u32[]{:S(2)}) copy-start(bf16[1,2,4,4096]{3,2,1,0:T(4,128)(2,1)} %copy-done.9) | copy-start | bytes 196612
  688.1 166.2 %copy-start.12 = (bf16[1,2,4,4096]{3,2,1,0:T(4,128)(2,1)S(1)}, bf16[1,2,4,4096]{3,2,1,0:T(4,128)(2,1)}, u32[]{:S(2)}) copy-start(bf16[1,2,4,4096]{3,2,1,0:T(4,128)(2,1)} %copy-done.11) | copy-start | bytes 196612
  688.1 166.2 %copy-start.14 = (bf16[1,2,4,4096]{3,2,1,0:T(4,128)(2,1)S(1)}, bf16[1,2,4,4096]{3,2,1,0:T(4,128)(2,1)}, u32[]{:S(2)}) copy-start(bf16[1,2,4,4096]{3,2,1,0:T(4,128)(2,1)} %copy-done.13) | copy-start | bytes 196612
  688.1 166.2 %copy-start.16 = (bf16[1,2,4,4096]{3,2,1,0:T(4,128)(2,1)S(1)}, bf16[1,2,4,4096]{3,2,1,0:T(4,128)(2,1)}, u32[]{:S(2)}) copy-start(bf16[1,2,4,4096]{3,2,1,0:T(4,128)(2,1)} %copy-done.15) | copy-start | bytes 196612
  688.1 166.2 %copy-start.62 = (f32[4096]{0:T(1024)S(1)}, f32[4096]{0:T(1024)}, u32[]{:S(2)}) copy-start(f32[4096]{0:T(1024)} %param.48) | copy-start | bytes 49156
  (44 other events, 383.2 us)
Sparse Core Ops, SparseCore 0:
  8.9 204.2 all-gather.9
  511.8 23.4 all-gather.13
  545.3 23.6 all-gather.15
  587.7 23.8 all-gather.17
  636.4 23.4 all-gather.11
  692.0 158.2 all-reduce.8
where the time goes:
time: 875 us; the launch traced here: 863 us
  local copies, waits for them, and re-layouts  234 us (27%)
  matrix products  204 us (23%)
  blocking collectives  195 us (22%)
  waiting for transfers between devices  158 us (18%)
  other arithmetic  55.1 us (6%)
  between operations  16 us (2%)
    unnamed x7, waiting for transfers between devices  158 us
    all_gather x4, blocking collectives, on_device(): gathered_rows = lax.all_gather(normed, 'tensor', axis=1, tiled=True)  128 us
    unnamed x147, local copies, waits for them, and re-layouts  45.4 us
    all_gather x8, blocking collectives, joined_2(): gathered = jax.tree.map(lambda a: lax.all_gather(a, axis), part)  43.2 us
    dot_general x4, matrix products, on_device(): jnp.einsum('brnd,rtnd->brnt', own_heads, prompt_keys, preferred_element_t...  41.9 us
    dot_general x4, matrix products, on_device(): jnp.einsum('brf,fd->rbd', hidden, down_weight, preferred_element_type=jnp...  37.9 us
    dot_general x4, matrix products, on_device(): jnp.einsum('brd,dc->brc', gathered_rows, qkv_flat, preferred_element_type...  35 us
    dot_general x4, matrix products, on_device(): jnp.einsum('brnt,rtnd->brnd', prompt_weights, prompt_values, preferred_el...  32.6 us
  transfers between devices with their start and end apart: 6, of which 1 were waited for; matrix products, arithmetic and copies ran while one was open for 37% of the time, Pallas kernels for 0%

commit v1 on v0

--- a/solution.py
+++ b/solution.py
@@ -3,6 +3,8 @@
 import jax
 import jax.numpy as jnp
 from jax import lax
+from jax.experimental import pallas as pl
+from jax.experimental.pallas import tpu as pltpu
 from jax.sharding import PartitionSpec as P
 
 HDIM = 256
@@ -90,7 +92,7 @@
     return (prompt_scores, chain_scores)
 
 
-def on_device(
+def stepwise(
     inputs,
     norm_gain,
     norm_bias,
@@ -257,6 +259,321 @@
     return jnp.stack(outputs, axis=0)
 
 
+VMEM_LIMIT = 58 * 2**20
+EXTRA = 128
+
+
+def dot32(a, b):
+    return jnp.dot(a, b, preferred_element_type=jnp.float32)
+
+
+def dot32_t(a, b):
+    return lax.dot_general(a, b, (((1,), (1,)), ((), ())), preferred_element_type=jnp.float32)
+
+
+def turn(tile, cosine, sine):
+    lane = lax.broadcasted_iota(jnp.int32, tile.shape, 1)
+    after = pltpu.roll(tile, HDIM - 1, 1)
+    before = pltpu.roll(tile, 1, 1)
+    return tile * cosine + jnp.where(lane % 2 == 0, after, before) * sine
+
+
+def project_kernel(tiles, x_ref, qkv_ref, in_ref, bias_ref, cos_ref, sin_ref, q_ref, kv_ref, hid_ref):
+    j = pl.program_id(0)
+
+    @pl.when(j < 2 * tiles)
+    def _():
+        turned = turn(dot32(x_ref[...], qkv_ref[0]), cos_ref[...], sin_ref[...]).astype(jnp.bfloat16)
+
+        @pl.when(j < tiles)
+        def _():
+            q_ref[...] = turned
+
+        @pl.when(j >= tiles)
+        def _():
+            kv_ref[0] = turned
+
+    @pl.when((j >= 2 * tiles) & (j < 3 * tiles))
+    def _():
+        kv_ref[0] = dot32(x_ref[...], qkv_ref[0]).astype(jnp.bfloat16)
+
+    @pl.when(j >= 3 * tiles)
+    def _():
+        hid_ref[...] = jax.nn.gelu(
+            dot32(x_ref[...], in_ref[...]) + bias_ref[...], approximate=True
+        ).astype(jnp.bfloat16)
+
+
+def project(rows, qkv3, in_weight, in_bias, cosine, sine):
+    count, width = rows.shape
+    columns = qkv3.shape[2]
+    units = in_weight.shape[1]
+    tiles = columns // HDIM
+    steps = 3 * tiles + units // HDIM
+    return pl.pallas_call(
+        lambda *refs: project_kernel(tiles, *refs),
+        grid=(steps,),
+        in_specs=[
+            pl.BlockSpec((count, width), lambda j: (0, 0)),
+            pl.BlockSpec(
+                (1, width, HDIM),
+                lambda j: (
+                    jnp.minimum(j, 3 * tiles - 1) // tiles,
+                    0,
+                    jnp.minimum(j, 3 * tiles - 1) % tiles,
+                ),
+            ),
+            pl.BlockSpec((width, HDIM), lambda j: (0, jnp.maximum(j - 3 * tiles, 0))),
+            pl.BlockSpec((1, HDIM), lambda j: (0, jnp.maximum(j - 3 * tiles, 0))),
+            pl.BlockSpec((count, HDIM), lambda j: (0, 0)),
+            pl.BlockSpec((count, HDIM), lambda j: (0, 0)),
+        ],
+        out_specs=[
+            pl.BlockSpec((count, HDIM), lambda j: (0, jnp.minimum(j, tiles - 1))),
+            pl.BlockSpec(
+                (1, count, HDIM),
+                lambda j: (
+                    jnp.clip(j - tiles, 0, 2 * tiles - 1) // tiles,
+                    0,
+                    jnp.clip(j - tiles, 0, 2 * tiles - 1) % tiles,
+                ),
+            ),
+            pl.BlockSpec((count, HDIM), lambda j: (0, jnp.maximum(j - 3 * tiles, 0))),
+        ],
+        out_shape=[
+            jax.ShapeDtypeStruct((count, columns), jnp.bfloat16),
+            jax.ShapeDtypeStruct((2, count, columns), jnp.bfloat16),
+            jax.ShapeDtypeStruct((count, units), jnp.bfloat16),
+        ],
+        compiler_params=pltpu.CompilerParams(vmem_limit_bytes=VMEM_LIMIT),
+    )(rows, qkv3, in_weight, in_bias.reshape(1, units), cosine, sine)
+
+
+def attend_kernel(
+    groups, beam_dev, heads, pages,
+    table_ref, length_ref, place_ref,
+    q_ref, kv_ref, old_ref, line_ref, *rest,
+):
+    page_refs = rest[:pages]
+    out_ref, mix_ref, peak_ref, total_ref = rest[pages:]
+    step = pl.program_id(0)
+    place = place_ref[0]
+    first = place * beam_dev
+    rows = q_ref.shape[2]
+    span = old_ref.shape[3]
+    page = page_refs[0].shape[2]
+    scale = HDIM ** (-0.5)
+
+    def query_rows(j):
+        parts = [q_ref[g, j].astype(jnp.float32) for g in range(groups)]
+        return jnp.concatenate(parts, axis=0).astype(jnp.bfloat16)
+
+    for j in range(groups):
+        query = query_rows(j)
+        line = line_ref[j]
+        new_lane = lax.broadcasted_iota(jnp.int32, (groups * rows, rows), 1)
+        new_ok = line[:, :rows] == first + new_lane % beam_dev
+        root = line[:, rows : rows + 1]
+        for h in range(heads):
+            cols = slice(h * HDIM, (h + 1) * HDIM)
+            scores = [
+                dot32_t(query[:, cols], old_ref[i, j, 0, :, cols]) * scale for i in range(beam_dev)
+            ]
+            oks = [jnp.broadcast_to(root == first + i, scores[i].shape) for i in range(beam_dev)]
+            scores.append(dot32_t(query[:, cols], kv_ref[0, j, :, cols]) * scale)
+            oks.append(new_ok)
+            values = [old_ref[i, j, 1, :, cols] for i in range(beam_dev)] + [kv_ref[1, j, :, cols]]
+            masked = [jnp.where(ok, s, NEG_FILL) for ok, s in zip(oks, scores)]
+            peak = masked[0].max(axis=1, keepdims=True)
+            for m in masked[1:]:
+                peak = jnp.maximum(peak, m.max(axis=1, keepdims=True))
+            total = 0.0
+            mix = 0.0
+            for m, ok, v in zip(masked, oks, values):
+                weights = jnp.where(ok, jnp.exp(m - peak), 0.0)
+                total = total + weights.sum(axis=1, keepdims=True)
+                mix = mix + dot32(weights.astype(jnp.bfloat16), v)
+            mix_ref[j, :, cols] = mix
+            peak_ref[j, h] = jnp.broadcast_to(peak, peak_ref.shape[2:])
+            total_ref[j, h] = jnp.broadcast_to(total, total_ref.shape[2:])
+
+    query = query_rows(place)
+    for h in range(heads):
+        cols = slice(h * HDIM, (h + 1) * HDIM)
+        masked = []
+        oks = []
+        for p in range(pages):
+            s = dot32_t(query[:, cols], page_refs[p][0, 0, :, cols]) * scale
+            ok = lax.broadcasted_iota(jnp.int32, s.shape, 1) + p * page < length_ref[step]
+            masked.append(jnp.where(ok, s, NEG_FILL))
+            oks.append(ok)
+        old_peak = peak_ref[place, h][:, :1]
+        peak = old_peak
+        for m in masked:
+            peak = jnp.maximum(peak, m.max(axis=1, keepdims=True))
+        factor = jnp.exp(old_peak - peak)
+        total = total_ref[place, h][:, :1] * factor
+        mix = mix_ref[place, :, cols] * factor
+        for p in range(pages):
+            weights = jnp.where(oks[p], jnp.exp(masked[p] - peak), 0.0)
+            total = total + weights.sum(axis=1, keepdims=True)
+            mix = mix + dot32(weights.astype(jnp.bfloat16), page_refs[p][0, 1, :, cols])
+        mix_ref[place, :, cols] = mix
+        peak_ref[place, h] = jnp.broadcast_to(peak, peak_ref.shape[2:])
+        total_ref[place, h] = jnp.broadcast_to(total, total_ref.shape[2:])
+
+    lane = lax.broadcasted_iota(jnp.int32, (groups * rows, EXTRA), 1)
+    columns = heads * HDIM
+    for j in range(groups):
+        extra = jnp.zeros((groups * rows, EXTRA), jnp.float32)
+        for h in range(heads):
+            cols = slice(h * HDIM, (h + 1) * HDIM)
+            total = total_ref[j, h]
+            held = total > 0.0
+            safe = jnp.where(held, total, 1.0)
+            level = jnp.where(held, peak_ref[j, h] + jnp.log(safe), NEG_FILL)
+            top = level.astype(jnp.bfloat16).astype(jnp.float32)
+            middle = (level - top).astype(jnp.bfloat16).astype(jnp.float32)
+            low = level - top - middle
+            extra = jnp.where(lane == 3 * h, top, extra)
+            extra = jnp.where(lane == 3 * h + 1, middle, extra)
+            extra = jnp.where(lane == 3 * h + 2, low, extra)
+            mixed = mix_ref[j, :, cols] / safe[:, :1]
+            for g in range(groups):
+                out_ref[g, j, :, cols] = mixed[g * rows : (g + 1) * rows].astype(jnp.bfloat16)
+        for g in range(groups):
+            out_ref[g, j, :, columns:] = extra[g * rows : (g + 1) * rows].astype(jnp.bfloat16)
+
+
+def attend(query_all, kv, old_cache, line, page_pool, table, lengths, place):
+    groups, requests, rows, columns = query_all.shape
+    beam_dev, _, _, span, _ = old_cache.shape
+    pages = table.shape[1]
+    page = page_pool.shape[2]
+    heads = columns // HDIM
+    many = groups * rows
+
+    def page_spec(p):
+        return pl.BlockSpec(
+            (1, 2, page, columns), lambda i, table, *_: (table[i * pages + p], 0, 0, 0)
+        )
+
+    return pl.pallas_call(
+        lambda *refs: attend_kernel(groups, beam_dev, heads, pages, *refs),
+        grid_spec=pltpu.PrefetchScalarGridSpec(
+            num_scalar_prefetch=3,
+            grid=(requests // groups,),
+            in_specs=[
+                pl.BlockSpec((groups, groups, rows, columns), lambda i, *_: (0, i, 0, 0)),
+                pl.BlockSpec((2, groups, rows, columns), lambda i, *_: (0, i, 0, 0)),
+                pl.BlockSpec((beam_dev, groups, 2, span, columns), lambda i, *_: (0, i, 0, 0, 0)),
+                pl.BlockSpec((groups, many, line.shape[2]), lambda i, *_: (i, 0, 0)),
+            ]
+            + [page_spec(p) for p in range(pages)],
+            out_specs=pl.BlockSpec(
+                (groups, groups, rows, columns + EXTRA), lambda i, *_: (0, i, 0, 0)
+            ),
+            scratch_shapes=[
+                pltpu.VMEM((groups, many, columns), jnp.float32),
+                pltpu.VMEM((groups, heads, many, EXTRA), jnp.float32),
+                pltpu.VMEM((groups, heads, many, EXTRA), jnp.float32),
+            ],
+        ),
+        out_shape=jax.ShapeDtypeStruct((groups, requests, rows, columns + EXTRA), jnp.bfloat16),
+        compiler_params=pltpu.CompilerParams(vmem_limit_bytes=VMEM_LIMIT),
+    )(table.reshape(-1), lengths, place, query_all, kv, old_cache, line, *[page_pool] * pages)
+
+
+def lineage_table(parents, groups, beam_dev):
+    steps, beams, requests = parents.shape
+    beam_ids = jnp.broadcast_to(jnp.arange(beams)[:, None], (beams, requests))
+    every = []
+    for step in range(steps):
+        lineage = beam_ids
+        found = []
+        for back in range(step, -1, -1):
+            found.append(lineage)
+            hits = lineage[:, None, :] == jnp.arange(beams)[None, :, None]
+            lineage = jnp.sum(jnp.where(hits, parents[back][None], 0), axis=1)
+        found = found[::-1] + [jnp.full_like(beam_ids, -1)] * (steps - 1 - step)
+        lanes = [f for f in found for _ in range(beam_dev)]
+        every.append(jnp.stack(lanes + [lineage], axis=-1))
+    table = jnp.stack(every, axis=0).reshape(steps, groups, beam_dev, requests, -1)
+    table = jnp.transpose(table, (3, 1, 0, 2, 4))
+    return table.reshape(requests, groups * steps * beam_dev, -1)
+
+
+def rotary_tables(prompt_length, history, steps, beam_dev):
+    requests = prompt_length.shape[0]
+    lane = jnp.arange(HDIM)
+    doubled = lane - lane % 2
+    frequency = jnp.where(
+        doubled < ROT, jnp.exp(-doubled.astype(jnp.float32) / ROT * math.log(10000.0)), 0.0
+    )
+    position = (prompt_length[:, None] + history + jnp.arange(steps)).astype(jnp.float32)
+    angles = position[:, :, None] * frequency
+    sign = jnp.where(lane % 2 == 0, -1.0, 1.0)
+    shape = (requests, steps, beam_dev, HDIM)
+
+    def spread(table):
+        return jnp.broadcast_to(table[:, :, None], shape).reshape(-1, HDIM)
+
+    return spread(jnp.cos(angles)), spread(jnp.sin(angles) * sign)
+
+
+def together(
+    inputs, norm_gain, norm_bias, qkv_weight, out_weight, in_weight, in_bias, down_weight,
+    down_bias, page_pool, old_cache, page_table, prompt_length, parents,
+):
+    place = lax.axis_index("batch")
+    groups = lax.axis_size("batch")
+    tensors = lax.axis_size("tensor")
+    steps, beam_dev, own_requests, width = inputs.shape
+    requests, pages = page_table.shape
+    columns = qkv_weight.shape[2]
+    heads = columns // HDIM
+    rows = steps * beam_dev
+    cosine, sine = rotary_tables(prompt_length, old_cache.shape[3], steps, beam_dev)
+    line = lineage_table(parents, groups, beam_dev)
+    own = jnp.arange(requests // groups) * groups + place
+    table = jnp.take(page_table, own, axis=0) - place * page_pool.shape[0]
+    lengths = jnp.take(prompt_length, own, axis=0)
+    current = jnp.transpose(inputs, (2, 0, 1, 3)).reshape(own_requests * rows, width)
+    normed = normalize(current, norm_gain, norm_bias).astype(jnp.bfloat16)
+    gathered = lax.all_gather(normed, "tensor", axis=0, tiled=True)
+    query, kv, hidden = project(
+        gathered, jnp.transpose(qkv_weight, (1, 0, 2)), in_weight, in_bias, cosine, sine
+    )
+    query_all = lax.all_gather(query, "batch").reshape(groups, requests, rows, columns)
+    partial = attend(
+        query_all, kv.reshape(2, requests, rows, columns), old_cache, line, page_pool, table,
+        lengths, place[None],
+    )
+    landed = lax.all_to_all(
+        partial.reshape(groups, requests * rows, columns + EXTRA), "batch", 0, 0
+    )
+    levels = landed[:, :, columns : columns + 3 * heads].astype(jnp.float32)
+    levels = levels.reshape(groups, requests * rows, heads, 3).sum(axis=-1)
+    shares = jnp.exp(levels - levels.max(axis=0))
+    shares = shares / shares.sum(axis=0)
+    attention = sum(
+        landed[g, :, :columns].astype(jnp.float32) * jnp.repeat(shares[g], HDIM, axis=1)
+        for g in range(groups)
+    ).astype(jnp.bfloat16)
+    update = dot32(attention, out_weight) + dot32(hidden, down_weight)
+    update = update.astype(jnp.bfloat16).reshape(tensors, own_requests * rows, width)
+    shared = lax.all_to_all(update, "tensor", 0, 0)
+    result = current.astype(jnp.float32) + shared.astype(jnp.float32).sum(axis=0) + down_bias
+    return jnp.transpose(result.reshape(own_requests, steps, beam_dev, width), (1, 2, 0, 3))
+
+
+def on_device(*arrays):
+    columns = arrays[3].shape[2]
+    if columns % HDIM:
+        return stepwise(*arrays)
+    return together(*arrays)
+
+
 def solution(mesh):
     in_specs = (
         P(None, "batch", "tensor", None),

time: 875 us -> 214 us (0.24); the launches traced: 863 us -> 214 us
  local copies, waits for them, and re-layouts: 234 us -> 9.44 us
  matrix products: 204 us -> 12.4 us
  blocking collectives: 195 us -> 53.6 us
  waiting for transfers between devices: 158 us -> 69.3 us
  other arithmetic: 55.1 us -> 8.99 us
  Pallas kernels: 0 us -> 42.6 us
    all_gather x16 -> x0, blocking collectives: 195 us -> none  [the longest x4 128 us: on_device(): gathered_rows = lax.all_gather(normed, 'tensor', axis=1, tiled=True)]
    dot_general x36 -> x2, matrix products: 204 us -> 12.4 us  [dot32(): return jnp.dot(a, b, preferred_element_type=jnp.float32)]
    unnamed x7 -> x2, waiting for transfers between devices: 158 us -> 0.03 us
    another operation x17 -> x2, local copies, waits for them, and re-layouts: 65.8 us -> 0.02 us  [lineage_table(): every.append(jnp.stack(lanes + [lineage], axis=-1))]
    all_gather x5 -> x2, waiting for transfers between devices: 0.08 us -> 59.7 us  [the longest x1 46.5 us: together(): gathered = lax.all_gather(normed, 'tensor', axis=0, tiled=True)]
    all_to_all x0 -> x1, blocking collectives: none -> 53.6 us  [together(): shared = lax.all_to_all(update, 'tensor', 0, 0)]
    unnamed x147 -> x33, local copies, waits for them, and re-layouts: 45.4 us -> 0.26 us
    pallas_call x0 -> x2, Pallas kernels: none -> 42.6 us  [the longest x1 26.8 us: attend(): pl.pallas_call(lambda *refs: attend_kernel(groups, beam_dev, heads, pages...]
  transfers between devices with their start and end apart: 6 -> 3, of which waited for: 1 -> 3; matrix products, arithmetic and copies ran while one was open for 37% -> 7% of each run, Pallas kernels for 0% -> 0%
where the time goes in v1:
time: 214 us
  waiting for transfers between devices  69.3 us (32%)
  blocking collectives  53.6 us (25%)
  Pallas kernels  42.6 us (20%)
  between operations  13.7 us (6%)
  matrix products  12.4 us (6%)
  local copies, waits for them, and re-layouts  9.44 us (4%)
  other arithmetic  8.99 us (4%)
  starting transfers between devices  3.58 us (2%)
    all_to_all x1, blocking collectives, together(): shared = lax.all_to_all(update, 'tensor', 0, 0)  53.6 us
    all_gather x1, waiting for transfers between devices, together(): gathered = lax.all_gather(normed, 'tensor', axis=0, tiled=True)  46.5 us
    pallas_call x1, Pallas kernels, attend(): pl.pallas_call(lambda *refs: attend_kernel(groups, beam_dev, heads, pages...  26.8 us
    pallas_call x1, Pallas kernels, project(): pl.pallas_call(lambda *refs: project_kernel(tiles, *refs), grid=(steps,),...  15.7 us
    all_gather x1, waiting for transfers between devices, together(): lax.all_gather(query, 'batch').reshape(groups, requests, rows, columns)  13.2 us
    dot_general x2, matrix products, dot32(): return jnp.dot(a, b, preferred_element_type=jnp.float32)  12.4 us
    all_to_all x1, waiting for transfers between devices, together(): lax.all_to_all(partial.reshape(groups, requests * rows, columns + EXTRA),...  9.58 us
  transfers between devices with their start and end apart: 3, of which 3 were waited for; matrix products, arithmetic and copies ran while one was open for 7% of the time, Pallas kernels for 0%

profile of v1, /device:TPU:0, one launch (start us, length us, event | category | flops | bytes accessed | tf_op | source)
XLA Modules:
  0.0 213.6 jit_solution(726427933059138937)
XLA Ops:
  6.5 1.2 fusion.10
  7.7 1.3 multiply_reduce_fusion
  9.0 0.1 copy.53
  9.1 1.0 convert_bitcast_fusion
  10.1 0.1 copy.54
  10.2 0.1 rsqrt.12
  10.3 0.1 div.19
  10.4 0.4 copy.52
  10.8 0.4 reshape.259
  11.2 1.6 add_convert_fusion
  13.0 0.6 gather_fusion.1
  13.6 0.6 gather_fusion
  14.3 0.7 sub.40.refs_0_
  15.1 1.1 fusion.11
  16.3 0.9 reshape.247.refs_5_
  17.3 0.9 reshape.246.refs_4_
  18.5 46.5 %all-gather.4.cloned.1.call-done.refs_0_ = bf16[256,4096]{1,0:T(8,128)(2,1)} async-done(((bf16[32,4096]{1,0:T(8,128)(2,1)}), bf16[256,4096]{1,0:T(8,128)(2,1)}) %all-gather.4.cloned.1.call-update) | async-done | bytes 2097168 | tf_op jit(solution)/shard_map/all_gather | solution.py:543
  65.0 15.7 %shard_map.136 = (bf16[256,512]{1,0:T(8,128)(2,1)}, bf16[2,256,512]{2,1,0:T(8,128)(2,1)}, bf16[256,1024]{1,0:T(8,128)(2,1)}) custom-call(bf16[256,4096]{1,0:T(8,128)(2,1)} %all-gather.4.cloned.1.call-done.refs_0_, bf16[3,4096,512]{2,1,0:T(8,128)(2,1)} %bitcast.86, bf16[4096,1024]{1,0:T(8,128)(2,1)} %refs_2_.1, f32[1,1024]{1,0:T(1,128)} %bitcast.113, ...), custom_call_target="tpu_custom_call" | custom-call | tf_op jit(solution)/shard_map/pallas_call | solution.py:313
  81.0 1.3 copy.55
  82.3 0.6 broadcast_select_fusion.refs_1_
  82.9 13.2 %all-gather.6.cloned.1.call-done = bf16[1024,512]{1,0:T(8,128)(2,1)} async-done(((bf16[256,512]{1,0:T(8,128)(2,1)}), bf16[1024,512]{1,0:T(8,128)(2,1)}) %all-gather.6.cloned.1.call-update) | async-done | bytes 1048592 | tf_op jit(solution)/shard_map/all_gather | solution.py:547
  96.1 26.8 %shard_map.137 = bf16[4,32,8,640]{3,2,1,0:T(8,128)(2,1)} custom-call(s32[32]{0:T(128)} %sub.40.refs_0_, s32[8]{0:T(128)} %broadcast_select_fusion.refs_1_, s32[1]{0:T(128)} %bitcast.2.refs_2_, bf16[4,32,8,512]{3,2,1,0:T(8,128)(2,1)} %bitcast.90, bf16[2,32,8,512]{3,2,1,0:T(8,128)(2,1)} %bitcast.91, bf16[2,32,2,64,512]{4,3,2,1,0:T(8,128)(2,1)} %refs_5_.1, ...), custom_call_target="tpu_custom_call" | custom-call | tf_op jit(solution)/shard_map/pallas_call | solution.py:461
  122.9 2.5 %copy.56 = bf16[4,256,640]{1,2,0:T(8,128)(2,1)} copy(bf16[4,256,640]{2,1,0:T(8,128)(2,1)} %bitcast.88) | data formatting | bytes 2621440 | tf_op jit(solution)/shard_map/reshape | solution.py:553
  125.4 3.5 %all-to-all-start = ((bf16[4,256,640]{1,2,0:T(8,128)(2,1)}), bf16[4,256,640]{1,2,0:T(8,128)(2,1)S(1)}, u32[]{:S(2)}, u32[]{:S(2)}) async-start(bf16[4,256,640]{1,2,0:T(8,128)(2,1)} %copy.56), calls=%async_computation | async-start | bytes 2621440 | tf_op jit(solution)/shard_map/all_to_all | solution.py:552
  129.0 7.6 %fusion.15 = f32[256,4096]{1,0:T(8,128)} fusion(bf16[256,1024]{1,0:T(8,128)(2,1)S(1)} %copy-done.5, bf16[1024,4096]{1,0:T(8,128)(2,1)} %param.21), kind=kOutput, calls=%fused_computation.105 | convolution fusion | flops 2147483648 | bytes 13107200 | tf_op jit(solution)/shard_map/dot_general | solution.py:267
  136.6 9.6 %all-to-all-done = bf16[4,256,640]{1,2,0:T(8,128)(2,1)S(1)} async-done(((bf16[4,256,640]{1,2,0:T(8,128)(2,1)}), bf16[4,256,640]{1,2,0:T(8,128)(2,1)S(1)}, u32[]{:S(2)}, u32[]{:S(2)}) %all-to-all-start) | async-done | bytes 1310752 | tf_op jit(solution)/shard_map/all_to_all | solution.py:552
  146.4 0.2 fusion.5
  146.6 4.8 %fusion.1 = bf16[256,4096]{1,0:T(8,128)(2,1)S(1)} fusion(f32[256,4096]{1,0:T(8,128)} %fusion.15, bf16[256,512]{0,1:T(8,128)(2,1)S(1)} %fusion.5, bf16[512,4096]{1,0:T(8,128)(2,1)} %param.18), kind=kOutput, calls=%fused_computation.4 | convolution fusion | flops 1075838976 | bytes 10747904 | tf_op jit(solution)/shard_map/dot_general | solution.py:267
  151.4 53.6 %all_to_all.10 = bf16[8,32,4096]{2,1,0:T(8,128)(2,1)S(1)} all-to-all(bf16[8,32,4096]{2,1,0:T(8,128)(2,1)S(1)} %bitcast.87), channel_id=1, replica_groups=mesh['batch'=4,'tensor'=8] {'tensor'}, dimensions={0} | all-to-all | bytes 4194304 | tf_op jit(solution)/shard_map/all_to_all | solution.py:565
  204.9 0.3 convert_reduce_fusion
  205.2 0.3 reduce_sum.152
  205.6 1.2 fusion.9
  (70 shorter events, 1.1 us)
Async XLA Ops:
  6.5 6.3 %copy-start.4 = (s32[32,4]{0,1:T(4,128)S(1)}, s32[32,4]{0,1:T(4,128)}, u32[]{:S(2)}) copy-start(s32[32,4]{0,1:T(4,128)} %param.25) | copy-start | bytes 1540
  6.5 6.5 %copy-start = (s32[32]{0:T(128)S(1)}, s32[32]{0:T(128)}, u32[]{:S(2)}) copy-start(s32[32]{0:T(128)} %param.26) | copy-start | bytes 388
  6.5 11.6 %copy-start.2 = (s32[4,8,32]{2,1,0:T(8,128)S(1)}, s32[4,8,32]{2,1,0:T(8,128)}, u32[]{:S(2)}) copy-start(s32[4,8,32]{2,1,0:T(8,128)} %param.27) | copy-start | bytes 12292
  6.5 58.4 %all-gather.4.cloned.1.call-start = ((), (), s32[]{:S(2)}) async-start(), calls=%async_computation.2 | async-start | bytes 2359296 | tf_op jit(solution)/shard_map/all_gather | solution.py:543
  12.8 83.3 %all-gather.6.cloned.1.call-start = ((), (), s32[]{:S(2)}) async-start(), calls=%async_computation.3 | async-start | bytes 1310720 | tf_op jit(solution)/shard_map/all_gather | solution.py:547
  122.9 6.0 %copy-start.5 = (bf16[256,1024]{1,0:T(8,128)(2,1)S(1)}, bf16[256,1024]{1,0:T(8,128)(2,1)}, u32[]{:S(2)}) copy-start(bf16[256,1024]{1,0:T(8,128)(2,1)} %get-tuple-element.10) | copy-start | bytes 1572868
  125.4 20.8 %all-to-all-start = ((bf16[4,256,640]{1,2,0:T(8,128)(2,1)}), bf16[4,256,640]{1,2,0:T(8,128)(2,1)S(1)}, u32[]{:S(2)}, u32[]{:S(2)}) async-start(bf16[4,256,640]{1,2,0:T(8,128)(2,1)} %copy.56), calls=%async_computation | async-start | bytes 2621440 | tf_op jit(solution)/shard_map/all_to_all | solution.py:552
  151.3 54.2 %copy-start.1 = (bf16[4,2,4,4096]{3,2,1,0:T(4,128)(2,1)S(1)}, bf16[4,2,4,4096]{3,2,1,0:T(4,128)(2,1)}, u32[]{:S(2)}) copy-start(bf16[4,2,4,4096]{3,2,1,0:T(4,128)(2,1)} %param.14) | copy-start | bytes 786436
  151.4 54.2 %copy-start.3 = (f32[4096]{0:T(1024)S(1)}, f32[4096]{0:T(1024)}, u32[]{:S(2)}) copy-start(f32[4096]{0:T(1024)} %param.22) | copy-start | bytes 49156
Sparse Core Ops, SparseCore 0:
  12.9 51.9 all-gather.3
  80.9 15.1 all-gather.5

commit v2 on v1

--- a/solution.py
+++ b/solution.py
@@ -363,6 +363,7 @@
     span = old_ref.shape[3]
     page = page_refs[0].shape[2]
     scale = HDIM ** (-0.5)
+    old_lane = lax.broadcasted_iota(jnp.int32, (groups * rows, beam_dev * span), 1)
 
     def query_rows(j):
         parts = [q_ref[g, j].astype(jnp.float32) for g in range(groups)]
@@ -376,13 +377,18 @@
         root = line[:, rows : rows + 1]
         for h in range(heads):
             cols = slice(h * HDIM, (h + 1) * HDIM)
+            old_keys = jnp.concatenate(
+                [old_ref[i, j, 0, :, cols] for i in range(beam_dev)], axis=0
+            )
+            old_values = jnp.concatenate(
+                [old_ref[i, j, 1, :, cols] for i in range(beam_dev)], axis=0
+            )
             scores = [
-                dot32_t(query[:, cols], old_ref[i, j, 0, :, cols]) * scale for i in range(beam_dev)
+                dot32_t(query[:, cols], old_keys) * scale,
+                dot32_t(query[:, cols], kv_ref[0, j, :, cols]) * scale,
             ]
-            oks = [jnp.broadcast_to(root == first + i, scores[i].shape) for i in range(beam_dev)]
-            scores.append(dot32_t(query[:, cols], kv_ref[0, j, :, cols]) * scale)
-            oks.append(new_ok)
-            values = [old_ref[i, j, 1, :, cols] for i in range(beam_dev)] + [kv_ref[1, j, :, cols]]
+            oks = [root == first + old_lane // span, new_ok]
+            values = [old_values, kv_ref[1, j, :, cols]]
             masked = [jnp.where(ok, s, NEG_FILL) for ok, s in zip(oks, scores)]
             peak = masked[0].max(axis=1, keepdims=True)
             for m in masked[1:]:
@@ -484,6 +490,128 @@
     )(table.reshape(-1), lengths, place, query_all, kv, old_cache, line, *[page_pool] * pages)
 
 
+def peers(axis):
+    count = lax.axis_size(axis)
+    me = lax.axis_index(axis)
+    beside = me + 1 - 2 * lax.rem(me, 2)
+    ahead = [lax.rem(me + 2 * k, count) for k in range(count // 2)]
+    behind = [lax.rem(me + count - 2 * k, count) for k in range(count // 2)]
+    return me, beside, ahead, behind
+
+
+def greet(axis, others):
+    barrier = pltpu.get_barrier_semaphore()
+    for other in others:
+        pl.semaphore_signal(
+            barrier, inc=1, device_id={axis: other}, device_id_type=pl.DeviceIdType.MESH
+        )
+    pl.semaphore_wait(barrier, len(others))
+
+
+def remote(axis, source, target, sent, landed, other):
+    return pltpu.make_async_remote_copy(
+        src_ref=source,
+        dst_ref=target,
+        send_sem=sent,
+        recv_sem=landed,
+        device_id={axis: other},
+        device_id_type=pl.DeviceIdType.MESH,
+    )
+
+
+def spread_kernel(axis, x_ref, out_ref, send_sem, land_sem, pass_sem, got_sem):
+    me, beside, ahead, behind = peers(axis)
+    half = len(ahead)
+    greet(axis, [beside] + ahead[1:])
+    sends = []
+    for k in range(1, half):
+        copy = remote(axis, x_ref, out_ref.at[me], send_sem.at[k], land_sem.at[k], ahead[k])
+        copy.start()
+        sends.append(copy)
+    passes = [remote(axis, x_ref, out_ref.at[me], pass_sem.at[0], got_sem.at[0], beside)]
+    passes[0].start()
+    out_ref[me] = x_ref[...]
+    for k in range(1, half):
+        sends[k - 1].wait_recv()
+        block = out_ref.at[behind[k]]
+        copy = remote(axis, block, block, pass_sem.at[k], got_sem.at[k], beside)
+        copy.start()
+        passes.append(copy)
+    for copy in passes:
+        copy.wait_recv()
+    for copy in sends + passes:
+        copy.wait_send()
+
+
+def spread_rows(block, axis, number):
+    count = lax.axis_size(axis)
+    return pl.pallas_call(
+        lambda *refs: spread_kernel(axis, *refs),
+        out_shape=jax.ShapeDtypeStruct((count,) + block.shape, block.dtype),
+        in_specs=[pl.BlockSpec(memory_space=pltpu.VMEM)],
+        out_specs=pl.BlockSpec(memory_space=pltpu.VMEM),
+        scratch_shapes=[pltpu.SemaphoreType.DMA((count // 2,))] * 4,
+        compiler_params=pltpu.CompilerParams(
+            collective_id=number, has_side_effects=True, vmem_limit_bytes=VMEM_LIMIT
+        ),
+    )(block)
+
+
+def total_kernel(
+    axis, part_ref, current_ref, bias_ref, out_ref, beside_ref, pair_ref, far_ref,
+    pass_sem, got_sem, send_sem, land_sem,
+):
+    me, beside, ahead, _ = peers(axis)
+    half = len(ahead)
+    count = lax.axis_size(axis)
+    greet(axis, [beside] + ahead[1:])
+    order = list(range(1, half)) + [0]
+    passes = {}
+    for k in order:
+        chunk = part_ref.at[lax.rem(beside + 2 * k, count)]
+        passes[k] = remote(axis, chunk, beside_ref.at[k], pass_sem.at[k], got_sem.at[k], beside)
+        passes[k].start()
+    sends = {}
+    for k in range(1, half):
+        passes[k].wait_recv()
+        pair = part_ref[ahead[k]].astype(jnp.float32) + beside_ref[k].astype(jnp.float32)
+        pair_ref[k] = pair.astype(pair_ref.dtype)
+        sends[k] = remote(
+            axis, pair_ref.at[k], far_ref.at[k], send_sem.at[k], land_sem.at[k], ahead[k]
+        )
+        sends[k].start()
+    passes[0].wait_recv()
+    out_ref[...] = (
+        part_ref[me].astype(jnp.float32)
+        + beside_ref[0].astype(jnp.float32)
+        + current_ref[...].astype(jnp.float32)
+        + bias_ref[...]
+    )
+    for k in range(1, half):
+        sends[k].wait_recv()
+        out_ref[...] += far_ref[k].astype(jnp.float32)
+    for k in order:
+        passes[k].wait_send()
+    for k in range(1, half):
+        sends[k].wait_send()
+
+
+def total_rows(parts, current, bias, axis, number):
+    count, rows, width = parts.shape
+    half = count // 2
+    return pl.pallas_call(
+        lambda *refs: total_kernel(axis, *refs),
+        out_shape=jax.ShapeDtypeStruct((rows, width), jnp.float32),
+        in_specs=[pl.BlockSpec(memory_space=pltpu.VMEM)] * 3,
+        out_specs=pl.BlockSpec(memory_space=pltpu.VMEM),
+        scratch_shapes=[pltpu.VMEM((half, rows, width), jnp.bfloat16)] * 3
+        + [pltpu.SemaphoreType.DMA((half,))] * 4,
+        compiler_params=pltpu.CompilerParams(
+            collective_id=number, has_side_effects=True, vmem_limit_bytes=VMEM_LIMIT
+        ),
+    )(parts, current, bias.reshape(1, width))
+
+
 def lineage_table(parents, groups, beam_dev):
     steps, beams, requests = parents.shape
     beam_ids = jnp.broadcast_to(jnp.arange(beams)[:, None], (beams, requests))
@@ -540,11 +668,11 @@
     lengths = jnp.take(prompt_length, own, axis=0)
     current = jnp.transpose(inputs, (2, 0, 1, 3)).reshape(own_requests * rows, width)
     normed = normalize(current, norm_gain, norm_bias).astype(jnp.bfloat16)
-    gathered = lax.all_gather(normed, "tensor", axis=0, tiled=True)
+    gathered = spread_rows(normed, "tensor", 0).reshape(requests * rows, width)
     query, kv, hidden = project(
         gathered, jnp.transpose(qkv_weight, (1, 0, 2)), in_weight, in_bias, cosine, sine
     )
-    query_all = lax.all_gather(query, "batch").reshape(groups, requests, rows, columns)
+    query_all = spread_rows(query, "batch", 1).reshape(groups, requests, rows, columns)
     partial = attend(
         query_all, kv.reshape(2, requests, rows, columns), old_cache, line, page_pool, table,
         lengths, place[None],
@@ -562,14 +690,13 @@
     ).astype(jnp.bfloat16)
     update = dot32(attention, out_weight) + dot32(hidden, down_weight)
     update = update.astype(jnp.bfloat16).reshape(tensors, own_requests * rows, width)
-    shared = lax.all_to_all(update, "tensor", 0, 0)
-    result = current.astype(jnp.float32) + shared.astype(jnp.float32).sum(axis=0) + down_bias
+    result = total_rows(update, current, down_bias, "tensor", 2)
     return jnp.transpose(result.reshape(own_requests, steps, beam_dev, width), (1, 2, 0, 3))
 
 
 def on_device(*arrays):
     columns = arrays[3].shape[2]
-    if columns % HDIM:
+    if columns % HDIM or lax.axis_size("tensor") % 2 or lax.axis_size("batch") % 2:
         return stepwise(*arrays)
     return together(*arrays)
 

time: 214 us -> 179 us (0.84)
  Pallas kernels: 42.6 us -> 130 us
  waiting for transfers between devices: 69.3 us -> 9.55 us
  blocking collectives: 53.6 us -> 0 us
  between operations: 13.7 us -> 0.29 us
  local copies, waits for them, and re-layouts: 9.44 us -> 14.5 us
  other arithmetic: 8.99 us -> 6.36 us
    pallas_call x0 -> x3, Pallas kernels: none -> 89.1 us  [the longest x2 50.6 us: spread_rows(): pl.pallas_call(lambda *refs: spread_kernel(axis, *refs), out_shape=jax.Sh...]
    all_gather x2 -> x0, waiting for transfers between devices: 59.7 us -> none  [the longest x1 46.5 us: together(): gathered = lax.all_gather(normed, 'tensor', axis=0, tiled=True)]
    all_to_all x1 -> x0, blocking collectives: 53.6 us -> none  [together(): shared = lax.all_to_all(update, 'tensor', 0, 0)]
    reshape x0 -> x3, local copies, waits for them, and re-layouts: none -> 2.58 us  [the longest x2 2.48 us: together(): result.reshape(own_requests, steps, beam_dev, width)]
  transfers between devices with their start and end apart: 3 -> 1, of which waited for: 3 -> 1; matrix products, arithmetic and copies ran while one was open for 7% -> 4% of each run, Pallas kernels for 0% -> 0%
where the time goes in v2:
time: 179 us; the launch traced here: 178 us
  Pallas kernels  130 us (73%)
  local copies, waits for them, and re-layouts  14.5 us (8%)
  matrix products  13.8 us (8%)
  waiting for transfers between devices  9.55 us (5%)
  other arithmetic  6.36 us (4%)
  starting transfers between devices  3.54 us (2%)
    pallas_call x2, Pallas kernels, spread_rows(): pl.pallas_call(lambda *refs: spread_kernel(axis, *refs), out_shape=jax.Sh...  50.6 us
    pallas_call x1, Pallas kernels, total_rows(): pl.pallas_call(lambda *refs: total_kernel(axis, *refs), out_shape=jax.Sha...  38.5 us
    pallas_call x1, Pallas kernels, attend(): pl.pallas_call(lambda *refs: attend_kernel(groups, beam_dev, heads, pages...  25.1 us
    pallas_call x1, Pallas kernels, project(): pl.pallas_call(lambda *refs: project_kernel(tiles, *refs), grid=(steps,),...  15.8 us
    dot_general x2, matrix products, dot32(): return jnp.dot(a, b, preferred_element_type=jnp.float32)  13.8 us
    all_to_all x1, waiting for transfers between devices, together(): lax.all_to_all(partial.reshape(groups, requests * rows, columns + EXTRA),...  9.55 us
  transfers between devices with their start and end apart: 1, of which 1 were waited for; matrix products, arithmetic and copies ran while one was open for 4% of the time, Pallas kernels for 0%

profile of v2, /device:TPU:0, one launch (start us, length us, event | category | flops | bytes accessed | tf_op | source)
XLA Modules:
  0.0 178.0 jit_solution(7708944472933297622)
XLA Ops:
  0.0 1.1 convert_reduce_fusion
  1.2 0.1 copy.52
  1.3 0.1 copy.54
  1.4 0.1 copy.53
  1.5 0.7 broadcast_add_fusion
  2.2 1.3 gather_fusion.1
  3.5 0.5 broadcast_select_fusion.refs_1_
  4.0 1.3 fusion.5
  5.4 0.1 copy.56
  5.8 0.8 copy.50
  6.6 0.6 gather_fusion
  7.2 0.6 sub.40.refs_0_
  7.8 0.7 slice_bitcast_fusion.7
  9.0 1.1 fusion.10
  10.2 0.9 reshape.250.refs_5_
  11.2 0.9 reshape.249.refs_4_
  12.1 1.2 copy.51
  13.6 1.3 copy.57
  14.9 0.9 add_convert_fusion.refs_0_
  15.7 38.9 %shard_map.136 = bf16[8,32,4096]{2,1,0:T(8,128)(2,1)} custom-call(bf16[32,4096]{1,0:T(8,128)(2,1)} %add_convert_fusion.refs_0_), custom_call_target="tpu_custom_call" | custom-call | tf_op jit(solution)/shard_map/pallas_call | solution.py:548
  54.7 15.8 %shard_map.137 = (bf16[256,512]{1,0:T(8,128)(2,1)}, bf16[2,256,512]{2,1,0:T(8,128)(2,1)}, bf16[256,1024]{1,0:T(8,128)(2,1)}) custom-call(bf16[256,4096]{1,0:T(8,128)(2,1)} %bitcast.85, bf16[3,4096,512]{2,1,0:T(8,128)(2,1)} %bitcast.84, bf16[4096,1024]{1,0:T(8,128)(2,1)} %refs_2_.1, f32[1,1024]{1,0:T(1,128)} %bitcast.114, f32[256,256]{1,0:T(8,128)} %reshape.249.refs_4_, ...), custom_call_target="tpu_custom_call" | custom-call | tf_op jit(solution)/shard_map/pallas_call | solution.py:313
  70.5 11.6 %shard_map.138 = bf16[4,256,512]{2,1,0:T(8,128)(2,1)} custom-call(bf16[256,512]{1,0:T(8,128)(2,1)} %get-tuple-element.8.refs_0_), custom_call_target="tpu_custom_call" | custom-call | tf_op jit(solution)/shard_map/pallas_call | solution.py:548
  82.1 25.1 %shard_map.139 = bf16[4,32,8,640]{3,2,1,0:T(8,128)(2,1)} custom-call(s32[32]{0:T(128)} %sub.40.refs_0_, s32[8]{0:T(128)} %broadcast_select_fusion.refs_1_, s32[1]{0:T(128)} %bitcast.1.refs_2_, bf16[4,32,8,512]{3,2,1,0:T(8,128)(2,1)} %bitcast.88, bf16[2,32,8,512]{3,2,1,0:T(8,128)(2,1)} %bitcast.91, bf16[2,32,2,64,512]{4,3,2,1,0:T(8,128)(2,1)} %refs_5_.1, ...), custom_call_target="tpu_custom_call" | custom-call | tf_op jit(solution)/shard_map/pallas_call | solution.py:467
  107.2 2.5 %copy.58 = bf16[4,256,640]{1,2,0:T(8,128)(2,1)} copy(bf16[4,256,640]{2,1,0:T(8,128)(2,1)} %bitcast.87) | data formatting | bytes 2621440 | tf_op jit(solution)/shard_map/reshape | solution.py:681
  109.7 3.5 %all-to-all-start = ((bf16[4,256,640]{1,2,0:T(8,128)(2,1)}), bf16[4,256,640]{1,2,0:T(8,128)(2,1)S(1)}, u32[]{:S(2)}, u32[]{:S(2)}) async-start(bf16[4,256,640]{1,2,0:T(8,128)(2,1)} %copy.58), calls=%async_computation | async-start | bytes 2621440 | tf_op jit(solution)/shard_map/all_to_all | solution.py:680
  113.3 7.7 %fusion.14 = f32[256,4096]{1,0:T(8,128)} fusion(bf16[256,1024]{1,0:T(8,128)(2,1)S(1)} %copy-done.3, bf16[1024,4096]{1,0:T(8,128)(2,1)} %param.21), kind=kOutput, calls=%fused_computation.103 | convolution fusion | flops 2147483648 | bytes 13107200 | tf_op jit(solution)/shard_map/dot_general | solution.py:267
  121.0 9.6 %all-to-all-done = bf16[4,256,640]{1,2,0:T(8,128)(2,1)S(1)} async-done(((bf16[4,256,640]{1,2,0:T(8,128)(2,1)}), bf16[4,256,640]{1,2,0:T(8,128)(2,1)S(1)}, u32[]{:S(2)}, u32[]{:S(2)}) %all-to-all-start) | async-done | bytes 1310752 | tf_op jit(solution)/shard_map/all_to_all | solution.py:680
  130.7 0.2 fusion.7
  130.9 6.1 %fusion.1 = bf16[256,4096]{1,0:T(8,128)(2,1)} fusion(f32[256,4096]{1,0:T(8,128)} %fusion.14, bf16[256,512]{0,1:T(8,128)(2,1)S(1)} %fusion.7, bf16[512,4096]{1,0:T(8,128)(2,1)} %param.18), kind=kOutput, calls=%fused_computation.4 | convolution fusion | flops 1075838976 | bytes 10747904 | tf_op jit(solution)/shard_map/dot_general | solution.py:267
  137.0 38.5 %shard_map.140 = f32[32,4096]{1,0:T(8,128)} custom-call(bf16[8,32,4096]{2,1,0:T(8,128)(2,1)} %bitcast.86, bf16[32,4096]{1,0:T(8,128)(2,1)} %copy-done, f32[1,4096]{1,0:T(1,128)} %bitcast.105), custom_call_target="tpu_custom_call" | custom-call | tf_op jit(solution)/shard_map/pallas_call | solution.py:602
  175.5 1.3 reshape.263
  176.9 1.1 copy.70
  (63 shorter events, 1.3 us)
Async XLA Ops:
  0.0 14.9 %copy-start.1 = (f32[4096]{0:T(1024)S(1)}, f32[4096]{0:T(1024)}, u32[]{:S(2)}) copy-start(f32[4096]{0:T(1024)} %param.16) | copy-start | bytes 49156
  0.0 14.9 %copy-start.2 = (f32[4096]{0:T(1024)S(1)}, f32[4096]{0:T(1024)}, u32[]{:S(2)}) copy-start(f32[4096]{0:T(1024)} %param.15) | copy-start | bytes 49156
  13.5 57.0 %copy-start = (bf16[32,4096]{1,0:T(8,128)(2,1)}, bf16[32,4096]{1,0:T(8,128)(2,1)S(1)}, u32[]{:S(2)}) copy-start(bf16[32,4096]{1,0:T(8,128)(2,1)S(1)} %reshape.246.refs_1_) | copy-start | bytes 786436
  107.2 6.0 %copy-start.3 = (bf16[256,1024]{1,0:T(8,128)(2,1)S(1)}, bf16[256,1024]{1,0:T(8,128)(2,1)}, u32[]{:S(2)}) copy-start(bf16[256,1024]{1,0:T(8,128)(2,1)} %get-tuple-element.10) | copy-start | bytes 1572868
  109.7 20.8 %all-to-all-start = ((bf16[4,256,640]{1,2,0:T(8,128)(2,1)}), bf16[4,256,640]{1,2,0:T(8,128)(2,1)S(1)}, u32[]{:S(2)}, u32[]{:S(2)}) async-start(bf16[4,256,640]{1,2,0:T(8,128)(2,1)} %copy.58), calls=%async_computation | async-start | bytes 2621440 | tf_op jit(solution)/shard_map/all_to_all | solution.py:680
